TPU v7x, 32 devices: a whole 2x2x4 slice. The times are simulated.
32 devices in a mesh: beam: 2 (over x), gx: 16 (over z, y, core).
Axes of the slice: x: 2, y: 2, z: 4, core: 2. Of those that a mesh axis runs over, the one named last changes fastest.
Arguments:
- filterbank: bfloat16 [4096, 2048], P(('beam', 'gx')), parts along dimension 0, may hold values from -61 to 61
- chan_delay: int32 [16, 2048], P(None, 'gx'), may hold values from 0 to 7
- sub_delay: int32 [1536, 64], replicated, may hold values from 0 to 15
- widths: int32 [1536], replicated, may hold values from 1 to 16
Outputs:
- snr: float32 [3072, 2048], P('beam', 'gx'), parts along dimension 0
There are 2 independent parts, one for each index of `beam`. A program takes and returns all parts, laid end to end along the dimension named above; an argument that names none is the same for every part. Nothing has to cross between parts.
All inputs are finite; a program needn't handle non-finite values.
Results may differ from a plain program's by a relative error of at most 0.00059.
Values may be sent and summed in bfloat16 or wider, within the bound.
A program may use at most 128 MiB of HBM per device.

v0:
```python
import jax
import jax.numpy as jnp
from jax import lax
from jax.sharding import PartitionSpec as P

SUBCH = 32
DELAY_ONE = 8
DELAY_TWO = 16
WMAX = 16


def passed_along(block, axis, distance):
    devices = range(lax.axis_size(axis))
    route = [(i - distance, i) for i in devices if i - distance in devices]
    return lax.ppermute(block, axis, route)


def per_device(filterbank, chan_delay, sub_delay, widths):
    chan_count, samples = filterbank.shape
    groups = chan_delay.shape[0]
    device_count = lax.axis_size("gx")
    sub_count = chan_count // SUBCH
    slab_len = samples // device_count
    trials, band_count = sub_delay.shape
    per_group = trials // groups
    margin_len = DELAY_TWO + WMAX
    span_len = slab_len + WMAX
    padded = jnp.pad(filterbank, ((0, 0), (0, DELAY_ONE)))
    band_input = padded.reshape(sub_count, SUBCH, samples + DELAY_ONE)
    band_delays = jnp.transpose(chan_delay.reshape(groups, sub_count, SUBCH), (1, 0, 2))
    first_codes = jnp.arange(DELAY_ONE, dtype=jnp.int32)[None, :, None]

    def band_sum(inputs):
        band_rows, delay_rows = inputs
        stacked = jnp.stack(
            [band_rows[:, offset : offset + samples] for offset in range(DELAY_ONE)], 0
        )
        stacked = stacked.reshape(DELAY_ONE * SUBCH, samples)
        one_hot = (
            (delay_rows[:, None, :] == first_codes)
            .astype(jnp.bfloat16)
            .reshape(groups, DELAY_ONE * SUBCH)
        )
        return jnp.dot(one_hot, stacked, preferred_element_type=jnp.float32).astype(jnp.bfloat16)

    subbands = lax.map(band_sum, (band_input, band_delays))
    regrouped = lax.all_to_all(subbands, "gx", split_axis=2, concat_axis=0, tiled=True)
    following = passed_along(regrouped[:, :, :margin_len], "gx", -1)
    extended = jnp.concatenate([regrouped, following], 2)
    trial_delays = sub_delay.reshape(groups, per_group, band_count)
    second_codes = jnp.arange(DELAY_TWO, dtype=jnp.int32)[None, :, None]

    def group_series(inputs):
        group_index, delay_rows = inputs
        group_rows = lax.dynamic_index_in_dim(extended, group_index, 1, keepdims=False)
        stacked = jnp.stack(
            [group_rows[:, offset : offset + span_len] for offset in range(DELAY_TWO)], 0
        )
        stacked = stacked.reshape(DELAY_TWO * band_count, span_len)
        one_hot = (
            (delay_rows[:, None, :] == second_codes)
            .astype(jnp.bfloat16)
            .reshape(per_group, DELAY_TWO * band_count)
        )
        own_part = jnp.dot(one_hot, stacked[:, :slab_len], preferred_element_type=jnp.float32)
        tail_part = lax.dot_general(
            stacked[:, slab_len:],
            one_hot,
            (((0,), (1,)), ((), ())),
            preferred_element_type=jnp.float32,
        )
        return (own_part, tail_part)

    own_blocks, tail_blocks = lax.map(
        group_series, (jnp.arange(groups, dtype=jnp.int32), trial_delays)
    )
    own_series = own_blocks.reshape(trials, slab_len)
    tail_cols = jnp.transpose(tail_blocks, (0, 2, 1)).reshape(trials, WMAX)
    series = jnp.concatenate([own_series, tail_cols], 1)
    boxcar = jnp.zeros((trials, slab_len), jnp.float32)
    for offset in range(WMAX):
        boxcar = boxcar + jnp.where(
            offset < widths[:, None], series[:, offset : offset + slab_len], 0.0
        )
    totals, squares = lax.psum(
        (jnp.sum(own_series, axis=1), jnp.sum(own_series * own_series, axis=1)), "gx"
    )
    average = totals / samples
    variance = squares / samples - average * average
    width_float = widths.astype(jnp.float32)[:, None]
    return (boxcar - width_float * average[:, None]) / jnp.sqrt(
        width_float * (variance[:, None] + 1e-05)
    )


def solution(mesh):
    in_specs = (P(("beam", "gx"), None), P(None, "gx"), P(), P())
    out_specs = P("beam", "gx")
    return jax.shard_map(
        per_device, mesh=mesh, in_specs=in_specs, out_specs=out_specs, check_vma=False
    )
```

profile of v0, /device:TPU:0, one launch (start us, length us, event | category | flops | bytes accessed | tf_op | source)
XLA Modules:
  0.0 178.4 jit_solution(11185816409424602314)
XLA Ops:
  0.0 0.8 reshape.68
  0.8 1.1 pad.4
  1.9 4.6 %while.24 = (s32[]{:T(128)}, bf16[4,16,2048]{2,1,0:T(8,128)(2,1)S(1)}, s32[4,16,32]{2,0,1:T(4,128)S(1)}, bf16[4,32,2056]{2,1,0:T(8,128)(2,1)S(1)}, s32[]{:T(128)}) while((s32[]{:T(128)}, bf16[4,16,2048]{2,1,0:T(8,128)(2,1)S(1)}, s32[4,16,32]{2,0,1:T(4,128)S(1)}, bf16[4,32,2056]{2,1,0:T(8,128)(2,1)S(1)}, s32[]{:T(128)}) %tuple.66), condition=%wide.region_1.2_spmd.clone, body=%wide.region_0.1_spmd.clone.sunk | while | flops 16814080 | bytes 3486793 | solution.py:46
  2.7 0.3 fusion.95
  3.9 0.3 fusion.95
  5.0 0.3 fusion.95
  6.2 0.3 fusion.95
  6.5 1.4 copy.16
  7.8 2.1 %reshape.74 = bf16[16,2,4096]{2,1,0:T(2,128)(2,1)S(1)} reshape(bf16[2048,4,16]{2,1,0:T(4,128)(2,1)S(1)} %bitcast.225) | data formatting | bytes 524288
  10.0 17.2 %all_to_all.18 = bf16[16,2,4096]{2,1,0:T(2,128)(2,1)S(1)} all-to-all(bf16[16,2,4096]{2,1,0:T(2,128)(2,1)S(1)} %reshape.74), channel_id=1, replica_groups=mesh['beam'=2,'gx'=16] {'gx'}, dimensions={0} | all-to-all | bytes 524288 | tf_op jit(solution)/shard_map/all_to_all | solution.py:47
  27.2 1.4 reshape.75
  28.7 1.0 copy.17
  29.7 1.3 collective-permute-start
  31.3 1.9 %collective-permute-done = bf16[64,16,32]{2,0,1:T(8,128)(2,1)S(1)} collective-permute-done((bf16[64,16,32]{2,0,1:T(8,128)(2,1)S(1)}, bf16[64,16,32]{2,0,1:T(8,128)(2,1)S(1)}, u32[]{:S(2)}, u32[]{:S(2)}) %collective-permute-start) | collective-permute-done | bytes 65568 | tf_op jit(solution)/shard_map/ppermute | solution.py:15
  33.3 70.5 %while.25 = (s32[]{:T(128)}, f32[16,96,128]{2,1,0:T(8,128)S(1)}, f32[16,16,96]{2,1,0:T(8,128)S(1)}, s32[16,96,64]{1,0,2:T(8,128)S(1)}, s32[16]{0:T(128)S(1)}, /*...) while((s32[]{:T(128)}, f32[16,96,128]{2,1,0:T(8,128)S(1)}, ...), condition=%wide.region_3.4_spmd.clone, body=%wide.region_2.3_spmd.clone.sunk | while | flops 28409860 | bytes 2107547 | solution.py:74
  33.3 0.6 dynamic_slice.38
  37.1 0.3 fusion.100
  37.4 0.2 fusion.101
  37.7 0.6 dynamic_slice.38
  41.5 0.3 fusion.100
  41.9 0.2 fusion.101
  42.1 0.6 dynamic_slice.38
  45.9 0.3 fusion.100
  46.3 0.2 fusion.101
  46.5 0.6 dynamic_slice.38
  50.3 0.3 fusion.100
  50.7 0.2 fusion.101
  50.9 0.6 dynamic_slice.38
  54.8 0.3 fusion.100
  55.1 0.2 fusion.101
  55.3 0.6 dynamic_slice.38
  59.2 0.3 fusion.100
  59.5 0.2 fusion.101
  59.7 0.6 dynamic_slice.38
  63.6 0.3 fusion.100
  63.9 0.2 fusion.101
  64.1 0.6 dynamic_slice.38
  68.0 0.3 fusion.100
  68.3 0.2 fusion.101
  68.5 0.6 dynamic_slice.38
  72.4 0.3 fusion.100
  72.7 0.2 fusion.101
  72.9 0.6 dynamic_slice.38
  76.8 0.3 fusion.100
  77.1 0.2 fusion.101
  77.3 0.6 dynamic_slice.38
  81.2 0.3 fusion.100
  81.5 0.2 fusion.101
  81.7 0.6 dynamic_slice.38
  85.6 0.3 fusion.100
  85.9 0.2 fusion.101
  86.1 0.6 dynamic_slice.38
  90.0 0.3 fusion.100
  90.5 0.6 dynamic_slice.38
  94.4 0.3 fusion.100
  94.7 0.2 fusion.101
  95.0 0.6 dynamic_slice.38
  98.8 0.3 fusion.100
  99.4 0.6 dynamic_slice.38
  103.2 0.3 fusion.100
  103.8 0.6 fusion.66
  104.5 0.3 copy.19
  104.8 61.6 %all-reduce.1 = (f32[1536]{0:T(1024)S(1)}, f32[1536]{0:T(1024)S(1)}) all-reduce(f32[1536]{0:T(1024)S(1)} %reduce_sum.25, f32[1536]{0:T(1024)S(1)} %reduce_sum.23), channel_id=1, replica_groups=mesh['beam'=2,'gx'=16] {'gx'}, use_global_device_ids=true, to_apply=%region_7.8 | all-reduce | flops 3072 | bytes 24576 | tf_op jit(solution)/shard_map/psum | solution.py:85
  166.5 11.9 %fusion.25 = f32[1536,128]{1,0:T(8,128)} fusion(f32[1536,128]{1,0:T(8,128)S(1)} %bitcast.229, f32[1536,16]{1,0:T(8,128)S(1)} %bitcast.228, f32[1536]{0:T(1024)S(1)} %get-tuple-element.146, f32[1536]{0:T(1024)S(1)} %get-tuple-element.145, pred[1536]{0:T(1024)(128)(4,1)S(1)} %get-tuple-element.162, pred[1536]{0:T(1024)(128)(4,1)S(1)} %get-tuple-element.148, ...), kind=kLoop, calls=%fused_computation.100 | loop fusion | flops 9437184 | bytes 1708032 | tf_op jit(solution)/shard_map/div | solution.py:91
  (393 shorter events, 28.9 us)
Async XLA Ops:
  27.2 3.8 %copy-start.1 = (s32[1536]{0:T(1024)S(1)}, s32[1536]{0:T(1024)}, u32[]{:S(2)}) copy-start(s32[1536]{0:T(1024)} %param.11) | copy-start | bytes 18436
  27.2 3.8 %copy-start = (s32[1536,64]{0,1:T(8,128)S(1)}, s32[1536,64]{0,1:T(8,128)}, u32[]{:S(2)}) copy-start(s32[1536,64]{0,1:T(8,128)} %param.10) | copy-start | bytes 1179652
  29.7 3.4 %collective-permute-start = (bf16[64,16,32]{2,0,1:T(8,128)(2,1)S(1)}, bf16[64,16,32]{2,0,1:T(8,128)(2,1)S(1)}, u32[]{:S(2)}, u32[]{:S(2)}) collective-permute-start(bf16[64,16,32]{2,0,1:T(8,128)(2,1)S(1)} %bitcast.231), channel_id=1, source_target_pairs={{1,0},{2,1},{3,2},{4,3},{5,4},{6,5},{7,6},{8,7},{9,8},{10,9},{11,1... | collective-permute-start | bytes 196616 | tf_op jit(solution)/shard_map/ppermute | solution.py:15
where the time goes:
time: 179 us; the launch traced here: 178 us
  blocking collectives  78.9 us (44%)
  local copies, waits for them, and re-layouts  42.3 us (24%)
  loops' own time  28.1 us (16%)
  other arithmetic  16 us (9%)
  matrix products  9.83 us (5%)
  waiting for transfers between devices  1.88 us (1%)
    psum x1, blocking collectives, per_device(): lax.psum((jnp.sum(own_series, axis=1), jnp.sum(own_series * own_series, a...  61.6 us
    another operation x1, loops' own time, per_device(): lax.map(group_series, (jnp.arange(groups, dtype=jnp.int32), trial_delays))  27.8 us
    while x268, local copies, waits for them, and re-layouts  20.8 us
    all_to_all x1, blocking collectives, per_device(): lax.all_to_all(subbands, 'gx', split_axis=2, concat_axis=0, tiled=True)  17.2 us
    div x1, other arithmetic, per_device(): (boxcar - width_float * average[:, None]) / jnp.sqrt(width_float * (varia...  11.9 us
    dynamic_slice x32, local copies, waits for them, and re-layouts, per_device(): lax.map(group_series, (jnp.arange(groups, dtype=jnp.int32), trial_delays))  9.85 us
    dot_general x16, matrix products, group_series(): jnp.dot(one_hot, stacked[:, :slab_len], preferred_element_type=jnp.float32)  5 us
  transfers between devices with their start and end apart: 1, of which 1 were waited for; matrix products, arithmetic and copies ran while one was open for 0% of the time, Pallas kernels for 0%

commit v1 on v0

v1 whole, which is shorter than its diff:
```python
import functools
import jax
import jax.numpy as jnp
from jax import lax
from jax.experimental import pallas as pl
from jax.experimental.pallas import tpu as pltpu
from jax.sharding import PartitionSpec as P

SUBCH = 32
DELAY_ONE = 8
DELAY_TWO = 16
WMAX = 16
LANES = 128
ROWS = 16
PREBUILD_BYTES = 24 << 20
MESH = pl.DeviceIdType.MESH


def lane_index(rows):
    return lax.broadcasted_iota(jnp.int32, (rows, LANES), 1)


def shifted(here, after, offset):
    if offset == 0:
        return here
    mixed = jnp.where(lane_index(here.shape[0]) >= offset, here, after)
    return pltpu.roll(mixed, LANES - offset, 1)


def main_kernel(
    n,
    fb_ref,
    cd_ref,
    sd_ref,
    w_ref,
    box_ref,
    res_ref,
    send,
    recv,
    x_main,
    x_halo,
    lhs,
    parts,
    mine,
    result,
    final,
    send_sem,
    recv_sem,
    part_send,
    part_recv,
    final_send,
    final_recv,
):
    me = lax.axis_index("gx")
    groups = cd_ref.shape[0]
    bands_here = cd_ref.shape[1] // SUBCH
    trials, bands = sd_ref.shape
    per_group = trials // groups
    samples = fb_ref.shape[1]
    tiles = samples // LANES
    main_rows = bands_here * groups
    rep = max(1, LANES // bands)
    width_k = rep * bands
    steps = (DELAY_TWO + WMAX) // rep
    prebuilt = lhs.shape[0] == groups
    bf16, f32 = jnp.bfloat16, jnp.float32

    barrier = pltpu.get_barrier_semaphore()

    @pl.loop(1, n)
    def _(s):
        pl.semaphore_signal(
            barrier, inc=1, device_id={"gx": lax.rem(me + s, n)}, device_id_type=MESH
        )

    lane = lane_index(groups)
    delays = cd_ref[...]
    code = jnp.concatenate(
        [
            jnp.where((lane >= SUBCH * b) & (lane < SUBCH * (b + 1)), delays, -1)
            for b in range(bands_here)
        ],
        0,
    )
    choose = jnp.concatenate(
        [jnp.where(code == o, 1.0, 0.0).astype(bf16) for o in range(DELAY_ONE)], 1
    )

    def tile(j):
        return fb_ref[:, pl.ds(pl.multiple_of(j * LANES, LANES), LANES)]

    def put(j, block):
        send[j, 0:main_rows, :] = block.astype(bf16)
        packed = jnp.zeros((groups, LANES), f32)
        for b in range(bands_here):
            head = jnp.where(lane < 2 * ROWS, block[b * groups : (b + 1) * groups], 0.0)
            packed = packed + (head if b == 0 else pltpu.roll(head, 2 * ROWS * b, 1))
        send[lax.rem(j + n - 1, n), main_rows : main_rows + groups, :] = packed.astype(bf16)

    @pl.loop(0, tiles // 2)
    def _(pair):
        first, second = tile(2 * pair), tile(2 * pair + 1)
        third = tile(jnp.minimum(2 * pair + 2, tiles - 1))
        third = jnp.where(2 * pair + 2 < tiles, third, jnp.zeros_like(third))
        stacked = jnp.concatenate(
            [
                jnp.concatenate([shifted(first, second, o), shifted(second, third, o)], 1)
                for o in range(DELAY_ONE)
            ],
            0,
        )
        block = jnp.dot(choose, stacked, preferred_element_type=f32)
        put(2 * pair, block[:, :LANES])
        put(2 * pair + 1, block[:, LANES:])

    send[n - 1, main_rows : main_rows + groups, :] = jnp.zeros((groups, LANES), bf16)

    pl.semaphore_wait(barrier, n - 1)

    def slab_copy(s, source, target):
        return pltpu.make_async_remote_copy(
            src_ref=send.at[target],
            dst_ref=recv.at[source],
            send_sem=send_sem.at[s],
            recv_sem=recv_sem.at[source],
            device_id={"gx": target},
            device_id_type=MESH,
        )

    @pl.loop(1, n)
    def _(s):
        slab_copy(s, me, lax.rem(me + s, n)).start()

    recv[me] = send[me]

    def build(g, slot):
        rows = pl.ds(pl.multiple_of(g * per_group, per_group), per_group)
        own = sd_ref[rows, :]
        own = jnp.concatenate([own - h for h in range(rep)], 1)
        wide = w_ref[rows, :]
        if width_k > LANES:
            wide = jnp.concatenate([wide] * (width_k // LANES), 1)
        for p in range(steps):
            gap = p * rep - own
            columns = slice(p * width_k, (p + 1) * width_k)
            inside = jnp.where((gap >= 0) & (gap < wide), 1.0, 0.0)
            lhs[slot, 0:per_group, columns] = inside.astype(bf16)
            if p * rep < DELAY_TWO:
                lhs[slot, per_group : 2 * per_group, columns] = jnp.where(
                    gap == 0, 1.0, 0.0
                ).astype(bf16)

    if prebuilt:

        @pl.loop(0, groups)
        def _(g):
            build(g, g)

    own_rows = pl.ds(
        pl.multiple_of(jnp.minimum(me, groups - 1) * per_group, per_group), per_group
    )
    own_width = w_ref[own_rows, :].astype(f32).T[0:1, :]

    @pl.loop(1, n)
    def _(s):
        slab_copy(s, lax.rem(me + n - s, n), me).wait_recv()

    per_pack = ROWS // bands_here
    out_row = lax.broadcasted_iota(jnp.int32, (ROWS * groups, ROWS * groups), 0)
    in_row = lax.broadcasted_iota(jnp.int32, (ROWS * groups, ROWS * groups), 1)
    turn = jnp.where(
        in_row == (out_row & (ROWS - 1)) * groups + (out_row >> 4), 1.0, 0.0
    ).astype(bf16)

    @pl.loop(0, n // per_pack)
    def _(q):
        mains, halos = [], []
        for s in range(per_pack):
            mains.append(recv[q * per_pack + s, 0:main_rows, :])
            halo = recv[q * per_pack + s, main_rows : main_rows + groups, :]
            for b in range(bands_here):
                halos.append(halo if b == 0 else pltpu.roll(halo, LANES - 2 * ROWS * b, 1))
        block = jnp.concatenate(
            [jnp.concatenate(mains, 0), jnp.concatenate(halos, 0)], 1
        )
        turned = jnp.dot(turn, block, preferred_element_type=f32).astype(bf16)
        rows = pl.ds(pl.multiple_of(q * ROWS, ROWS), ROWS)
        for g in range(groups):
            x_main[g, rows, :] = turned[g * ROWS : (g + 1) * ROWS, :LANES]
            x_halo[g, rows, :] = turned[g * ROWS : (g + 1) * ROWS, LANES:]

    def part_copy(g, source):
        return pltpu.make_async_remote_copy(
            src_ref=mine.at[g],
            dst_ref=parts.at[source],
            send_sem=part_send.at[g],
            recv_sem=part_recv.at[source],
            device_id={"gx": g},
            device_id_type=MESH,
        )

    chunk = max(1, 256 // bands)

    @pl.loop(0, groups)
    def _(g):
        slot = g if prebuilt else 0
        if not prebuilt:
            build(g, 0)
        here, after = x_main[g], x_halo[g]
        both = jnp.zeros((2 * per_group, LANES), f32)
        upper = jnp.zeros((per_group, LANES), f32)
        for first in range(0, DELAY_TWO + WMAX, chunk):
            stacked = jnp.concatenate(
                [shifted(here, after, o) for o in range(first, first + chunk)], 0
            )
            columns = slice(first * bands, (first + chunk) * bands)
            if first < DELAY_TWO:
                both = both + jnp.dot(
                    lhs[slot, :, columns], stacked, preferred_element_type=f32
                )
            else:
                upper = upper + jnp.dot(
                    lhs[slot, 0:per_group, columns], stacked, preferred_element_type=f32
                )
        rows = pl.ds(pl.multiple_of(g * per_group, per_group), per_group)
        box_ref[rows, :] = both[:per_group] + upper
        turned = both[per_group:].T
        total = jnp.sum(turned, axis=0, keepdims=True)
        centred = turned - total / LANES
        mine[g, 0:1, 0:per_group] = total
        mine[g, 1:2, 0:per_group] = jnp.sum(centred * centred, axis=0, keepdims=True)

        @pl.when(g != me)
        def _():
            part_copy(g, me).start()

        @pl.when(g == me)
        def _():
            parts[me] = mine[g]

    def final_copy(s, source, target):
        return pltpu.make_async_remote_copy(
            src_ref=result,
            dst_ref=final.at[source],
            send_sem=final_send.at[s],
            recv_sem=final_recv.at[source],
            device_id={"gx": target},
            device_id_type=MESH,
        )

    def settle():
        @pl.loop(1, n)
        def _(s):
            part_copy(me, lax.rem(me + n - s, n)).wait_recv()

        totals = parts[:, 0, 0:per_group]
        squares = parts[:, 1, 0:per_group]
        average = jnp.sum(totals, axis=0, keepdims=True) / samples
        away = totals / LANES - average
        variance = (
            jnp.sum(squares, axis=0, keepdims=True)
            + LANES * jnp.sum(away * away, axis=0, keepdims=True)
        ) / samples
        result[0:1, 0:per_group] = own_width * average
        result[1:2, 0:per_group] = 1.0 / jnp.sqrt(own_width * (variance + 1e-05))

        @pl.loop(1, n)
        def _(s):
            final_copy(s, me, lax.rem(me + s, n)).start()

        final[me] = result[...]

        @pl.loop(1, n)
        def _(s):
            final_copy(s, me, lax.rem(me + s, n)).wait_send()

    if n > groups:
        pl.when(me < groups)(settle)
    else:
        settle()

    @pl.loop(0, groups)
    def _(g):
        @pl.when(g != me)
        def _():
            final_copy(1, g, me).wait_recv()
            part_copy(g, me).wait_send()

    res_ref[...] = final[...]

    @pl.loop(1, n)
    def _(s):
        slab_copy(s, me, lax.rem(me + s, n)).wait_send()


def norm_kernel(box_ref, res_ref, out_ref):
    groups = res_ref.shape[0]
    per_group = box_ref.shape[0] // groups
    for g in range(groups):
        rows = slice(g * per_group, (g + 1) * per_group)
        base, scale = (
            jnp.broadcast_to(res_ref[g, i : i + 1, :], (LANES, LANES)).T[:per_group]
            for i in range(2)
        )
        out_ref[rows, :] = (box_ref[rows, :] - base) * scale


def per_device(filterbank, chan_delay, sub_delay, widths):
    chan_count, samples = filterbank.shape
    groups = chan_delay.shape[0]
    n = lax.axis_size("gx")
    trials, bands = sub_delay.shape
    per_group = trials // groups
    bands_here = chan_count // SUBCH
    assert samples == n * LANES and n >= groups and chan_count == LANES
    message_rows = (bands_here + 1) * groups
    offsets = DELAY_TWO + WMAX
    slot_bytes = 2 * per_group * offsets * bands * 2
    slots = groups if groups * slot_bytes <= PREBUILD_BYTES else 1
    wide = jnp.broadcast_to(widths[:, None], (trials, LANES))
    bf16, f32 = jnp.bfloat16, jnp.float32
    vmem = pl.BlockSpec(memory_space=pltpu.VMEM)
    dma = pltpu.SemaphoreType.DMA
    boxcar, stats = pl.pallas_call(
        functools.partial(main_kernel, n),
        out_shape=(
            jax.ShapeDtypeStruct((trials, LANES), f32),
            jax.ShapeDtypeStruct((groups, 2, LANES), f32),
        ),
        in_specs=[vmem] * 4,
        out_specs=(vmem, vmem),
        scratch_shapes=[
            pltpu.VMEM((n, message_rows, LANES), bf16),
            pltpu.VMEM((n, message_rows, LANES), bf16),
            pltpu.VMEM((groups, bands, LANES), bf16),
            pltpu.VMEM((groups, bands, LANES), bf16),
            pltpu.VMEM((slots, 2 * per_group, offsets * bands), bf16),
            pltpu.VMEM((n, 2, LANES), f32),
            pltpu.VMEM((groups, 2, LANES), f32),
            pltpu.VMEM((2, LANES), f32),
            pltpu.VMEM((groups, 2, LANES), f32),
            dma((n,)),
            dma((n,)),
            dma((groups,)),
            dma((n,)),
            dma((n,)),
            dma((groups,)),
        ],
        compiler_params=pltpu.CompilerParams(
            collective_id=0, has_side_effects=True, vmem_limit_bytes=56 << 20
        ),
        name="dedisperse",
    )(filterbank, chan_delay, sub_delay, wide)
    return pl.pallas_call(
        norm_kernel,
        out_shape=jax.ShapeDtypeStruct((trials, LANES), f32),
        in_specs=[vmem] * 2,
        out_specs=vmem,
        name="normalise",
    )(boxcar, stats)


def solution(mesh):
    in_specs = (P(("beam", "gx"), None), P(None, "gx"), P(), P())
    out_specs = P("beam", "gx")
    return jax.shard_map(
        per_device, mesh=mesh, in_specs=in_specs, out_specs=out_specs, check_vma=False
    )
```

time: 179 us -> 39.9 us (0.22)
  blocking collectives: 78.9 us -> 0 us
  local copies, waits for them, and re-layouts: 42.3 us -> 3.31 us
  Pallas kernels: 0 us -> 36.4 us
  loops' own time: 28.1 us -> 0 us
  other arithmetic: 16 us -> 0 us
  matrix products: 9.83 us -> 0 us
  waiting for transfers between devices: 1.88 us -> 0 us
    psum x1 -> x0, blocking collectives: 61.6 us -> none  [per_device(): lax.psum((jnp.sum(own_series, axis=1), jnp.sum(own_series * own_series, a...]
    pallas_call x0 -> x2, Pallas kernels: none -> 36.4 us  [the longest x1 33.8 us: per_device(): pl.pallas_call(functools.partial(main_kernel, n), out_shape=(jax.ShapeDty...]
    another operation x2 -> x0, loops' own time: 28.1 us -> none  [the longest x1 27.8 us: per_device(): lax.map(group_series, (jnp.arange(groups, dtype=jnp.int32), trial_delays))]
    while x269 -> x0, local copies, waits for them, and re-layouts: 22.2 us -> none
    all_to_all x1 -> x0, blocking collectives: 17.2 us -> none  [per_device(): lax.all_to_all(subbands, 'gx', split_axis=2, concat_axis=0, tiled=True)]
    div x1 -> x0, other arithmetic: 11.9 us -> none  [per_device(): (boxcar - width_float * average[:, None]) / jnp.sqrt(width_float * (varia...]
    dynamic_slice x36 -> x0, local copies, waits for them, and re-layouts: 9.91 us -> none  [the longest x32 9.85 us: per_device(): lax.map(group_series, (jnp.arange(groups, dtype=jnp.int32), trial_delays))]
    dot_general x36 -> x0, matrix products: 9.83 us -> none  [the longest x16 5 us: group_series(): jnp.dot(one_hot, stacked[:, :slab_len], preferred_element_type=jnp.float32)]
  transfers between devices with their start and end apart: 1 -> 0, of which waited for: 1 -> 0; matrix products, arithmetic and copies ran while one was open for 0% -> 0% of each run, Pallas kernels for 0% -> 0%
where the time goes in v1:
time: 39.9 us; the launch traced here: 39.7 us
  Pallas kernels  36.4 us (91%)
  local copies, waits for them, and re-layouts  3.31 us (8%)
    pallas_call x1, Pallas kernels, per_device(): pl.pallas_call(functools.partial(main_kernel, n), out_shape=(jax.ShapeDty...  33.8 us
    pallas_call x1, Pallas kernels, per_device(): pl.pallas_call(norm_kernel, out_shape=jax.ShapeDtypeStruct((trials, LANES...  2.61 us
    unnamed x3, local copies, waits for them, and re-layouts  2.16 us
    broadcast_in_dim x1, local copies, waits for them, and re-layouts, per_device(): wide = jnp.broadcast_to(widths[:, None], (trials, LANES))  1.15 us

profile of v1, /device:TPU:0, one launch (start us, length us, event | category | flops | bytes accessed | tf_op | source)
XLA Modules:
  0.0 39.7 jit_solution(11295585783916020366)
XLA Ops:
  0.0 0.0 copy-start
  0.0 2.2 %copy.5.sd_ref = s32[1536,64]{1,0:T(8,128)} copy(s32[1536,64]{0,1:T(8,128)} %param.6) | data formatting | bytes 786432 | tf_op args[2]
  2.2 0.0 copy-done
  2.2 1.1 %broadcast_in_dim.2.w_ref = s32[1536,128]{1,0:T(8,128)} broadcast(s32[1536]{0:T(1024)S(1)} %copy-done), dimensions={0} | broadcast | bytes 792576 | tf_op jit(solution)/shard_map/broadcast_in_dim | solution.py:320
  3.3 33.8 %dedisperse.1 = (f32[1536,128]{1,0:T(8,128)}, f32[16,2,128]{2,1,0:T(2,128)}) custom-call(bf16[128,2048]{1,0:T(8,128)(2,1)} %fb_ref.1, s32[16,128]{1,0:T(8,128)} %cd_ref.1, s32[1536,64]{1,0:T(8,128)} %copy.5.sd_ref, s32[1536,128]{1,0:T(8,128)} %broadcast_in_dim.2.w_ref), custom_call_target="tpu_custom_call" | custom-call | tf_op jit(solution)/shard_map/dedisperse/pallas_call | solution.py:324
  37.1 2.6 %normalise.1 = f32[1536,128]{1,0:T(8,128)} custom-call(f32[1536,128]{1,0:T(8,128)} %get-tuple-element.7.box_ref, f32[16,2,128]{2,1,0:T(2,128)} %get-tuple-element.8.res_ref), custom_call_target="tpu_custom_call" | custom-call | tf_op jit(solution)/shard_map/normalise/pallas_call | solution.py:354
Async XLA Ops:
  0.0 2.2 %copy-start = (s32[1536]{0:T(1024)S(1)}, s32[1536]{0:T(1024)}, u32[]{:S(2)}) copy-start(s32[1536]{0:T(1024)} %param.7) | copy-start | bytes 18436

commit v2 on v1

v2 whole, which is shorter than its diff:
```python
import functools
import math
import jax
import jax.numpy as jnp
from jax import lax
from jax.experimental import pallas as pl
from jax.experimental.pallas import tpu as pltpu
from jax.sharding import PartitionSpec as P

SUBCH = 32
DELAY_ONE = 8
DELAY_TWO = 16
WMAX = 16
LANES = 128
ROWS = 16
PREBUILD_BYTES = 24 << 20
MESH = pl.DeviceIdType.MESH


def lane_index(rows):
    return lax.broadcasted_iota(jnp.int32, (rows, LANES), 1)


def shifted(here, after, offset):
    if offset == 0:
        return here
    mixed = jnp.where(lane_index(here.shape[0]) >= offset, here, after)
    return pltpu.roll(mixed, LANES - offset, 1)


def main_kernel(
    n,
    fb_in,
    cd_in,
    sd_in,
    w_in,
    box_ref,
    res_ref,
    fb_ref,
    cd_ref,
    sd_ref,
    w_ref,
    gaps,
    wide,
    width_rows,
    send,
    recv,
    x_main,
    x_halo,
    lhs,
    parts,
    mine,
    load_sem,
    send_sem,
    recv_sem,
    part_send,
    part_recv,
):
    me = lax.axis_index("gx")
    groups = cd_ref.shape[0]
    bands_here = cd_ref.shape[1] // SUBCH
    bands, trials = sd_ref.shape
    per_group = trials // groups
    samples = fb_ref.shape[1]
    tiles = samples // LANES
    main_rows = bands_here * groups
    rep = max(1, LANES // bands)
    width_k = rep * bands
    steps = (DELAY_TWO + WMAX) // rep
    prebuilt = lhs.shape[0] == groups
    bf16, f32 = jnp.bfloat16, jnp.float32

    barrier = pltpu.get_barrier_semaphore()

    @pl.loop(1, n)
    def _(s):
        pl.semaphore_signal(
            barrier, inc=1, device_id={"gx": lax.rem(me + s, n)}, device_id_type=MESH
        )

    loads = [
        pltpu.make_async_copy(source, target, load_sem.at[i])
        for i, (source, target) in enumerate(
            [(cd_in, cd_ref), (fb_in, fb_ref), (sd_in, sd_ref), (w_in, w_ref)]
        )
    ]
    for load in loads:
        load.start()

    loads[0].wait()
    lane = lane_index(groups)
    delays = cd_ref[...]
    code = jnp.concatenate(
        [
            jnp.where((lane >= SUBCH * b) & (lane < SUBCH * (b + 1)), delays, -1)
            for b in range(bands_here)
        ],
        0,
    )
    choose = jnp.concatenate(
        [jnp.where(code == o, 1.0, 0.0).astype(bf16) for o in range(DELAY_ONE)], 1
    )

    def tile(j):
        return fb_ref[:, pl.ds(pl.multiple_of(j * LANES, LANES), LANES)]

    def put(j, block):
        send[j, 0:main_rows, :] = block.astype(bf16)
        packed = jnp.zeros((groups, LANES), f32)
        for b in range(bands_here):
            head = jnp.where(lane < 2 * ROWS, block[b * groups : (b + 1) * groups], 0.0)
            packed = packed + (head if b == 0 else pltpu.roll(head, 2 * ROWS * b, 1))
        send[lax.rem(j + n - 1, n), main_rows : main_rows + groups, :] = packed.astype(bf16)

    loads[1].wait()

    @pl.loop(0, tiles // 2)
    def _(pair):
        first, second = tile(2 * pair), tile(2 * pair + 1)
        third = tile(jnp.minimum(2 * pair + 2, tiles - 1))
        third = jnp.where(2 * pair + 2 < tiles, third, jnp.zeros_like(third))
        stacked = jnp.concatenate(
            [
                jnp.concatenate([shifted(first, second, o), shifted(second, third, o)], 1)
                for o in range(DELAY_ONE)
            ],
            0,
        )
        block = jnp.dot(choose, stacked, preferred_element_type=f32)
        put(2 * pair, block[:, :LANES])
        put(2 * pair + 1, block[:, LANES:])

    send[n - 1, main_rows : main_rows + groups, :] = jnp.zeros((groups, LANES), bf16)

    pl.semaphore_wait(barrier, n - 1)

    def slab_copy(s, source, target):
        return pltpu.make_async_remote_copy(
            src_ref=send.at[target],
            dst_ref=recv.at[source],
            send_sem=send_sem.at[s],
            recv_sem=recv_sem.at[source],
            device_id={"gx": target},
            device_id_type=MESH,
        )

    @pl.loop(1, n)
    def _(s):
        slab_copy(s, me, lax.rem(me + s, n)).start()

    recv[me] = send[me]

    loads[2].wait()
    loads[3].wait()
    for first in range(0, trials, LANES):
        cut = slice(first, first + LANES)
        some = sd_ref[:, cut]
        gaps[cut, :] = jnp.concatenate([some - h for h in range(rep)], 0).T
        wide[cut, :] = jnp.broadcast_to(w_ref[cut].reshape(1, LANES), (LANES, LANES)).T
    for g in range(groups):
        row = wide[g * per_group : (g + 1) * per_group, :].astype(f32).T[0:1, :]
        width_rows[g : g + 1, 0:per_group] = row

    def build(g, slot):
        rows = pl.ds(pl.multiple_of(g * per_group, per_group), per_group)
        own, top = gaps[rows, :], wide[rows, :]
        if width_k > LANES:
            top = jnp.concatenate([top] * (width_k // LANES), 1)
        for p in range(steps):
            gap = p * rep - own
            columns = slice(p * width_k, (p + 1) * width_k)
            inside = jnp.where((gap >= 0) & (gap < top), 1.0, 0.0)
            lhs[slot, 0:per_group, columns] = inside.astype(bf16)
            if p * rep < DELAY_TWO:
                lhs[slot, per_group : 2 * per_group, columns] = jnp.where(
                    gap == 0, 1.0, 0.0
                ).astype(bf16)

    if prebuilt:

        @pl.loop(0, groups)
        def _(g):
            build(g, g)

    per_pack = ROWS // bands_here
    out_row = lax.broadcasted_iota(jnp.int32, (ROWS * groups, ROWS * groups), 0)
    in_row = lax.broadcasted_iota(jnp.int32, (ROWS * groups, ROWS * groups), 1)
    turn = jnp.where(
        in_row == (out_row & (ROWS - 1)) * groups + (out_row >> 4), 1.0, 0.0
    ).astype(bf16)

    @pl.loop(0, n // per_pack)
    def _(q):
        mains, halos = [], []
        for s in range(per_pack):
            source = q * per_pack + s

            @pl.when(source != me)
            def _():
                slab_copy(0, source, me).wait_recv()

            mains.append(recv[source, 0:main_rows, :])
            halo = recv[source, main_rows : main_rows + groups, :]
            for b in range(bands_here):
                halos.append(halo if b == 0 else pltpu.roll(halo, LANES - 2 * ROWS * b, 1))
        block = jnp.concatenate(
            [jnp.concatenate(mains, 0), jnp.concatenate(halos, 0)], 1
        )
        turned = jnp.dot(turn, block, preferred_element_type=f32).astype(bf16)
        rows = pl.ds(pl.multiple_of(q * ROWS, ROWS), ROWS)
        for g in range(groups):
            x_main[g, rows, :] = turned[g * ROWS : (g + 1) * ROWS, :LANES]
            x_halo[g, rows, :] = turned[g * ROWS : (g + 1) * ROWS, LANES:]

    chunk = max(1, 256 // bands)
    turns, _, _, turn_groups, _ = parts.shape

    def part_copy(c, s, source, target):
        return pltpu.make_async_remote_copy(
            src_ref=mine.at[c],
            dst_ref=parts.at[c, source],
            send_sem=part_send.at[c, s],
            recv_sem=part_recv.at[c, source],
            device_id={"gx": target},
            device_id_type=MESH,
        )

    def rows_of(g):
        return pl.ds(pl.multiple_of(g * per_group, per_group), per_group)

    def summed(g, rows, firsts):
        slot = g if prebuilt else 0
        if not prebuilt:
            build(g, 0)
        here, after = x_main[g], x_halo[g]
        total = jnp.zeros((rows, LANES), f32)
        for first in firsts:
            stacked = jnp.concatenate(
                [shifted(here, after, o) for o in range(first, first + chunk)], 0
            )
            columns = slice(first * bands, (first + chunk) * bands)
            total = total + jnp.dot(
                lhs[slot, 0:rows, columns], stacked, preferred_element_type=f32
            )
        return total

    for c in range(turns):

        @pl.loop(0, turn_groups)
        def _(r):
            g = c * turn_groups + r
            both = summed(g, 2 * per_group, range(0, DELAY_TWO, chunk))
            box_ref[rows_of(g), :] = both[:per_group]
            turned = both[per_group:].T
            total = jnp.sum(turned, axis=0, keepdims=True)
            centred = turned - total / LANES
            square = jnp.sum(centred * centred, axis=0, keepdims=True)
            mine[c, 0, pl.ds(r, 1), 0:per_group] = total
            mine[c, 1, pl.ds(r, 1), 0:per_group] = square

        @pl.loop(1, n)
        def _(s):
            part_copy(c, s, me, lax.rem(me + s, n)).start()

        parts[c, me] = mine[c]

    @pl.loop(0, groups)
    def _(g):
        upper = summed(g, per_group, range(DELAY_TWO, DELAY_TWO + WMAX, chunk))
        box_ref[rows_of(g), :] = box_ref[rows_of(g), :] + upper

    for c in range(turns):

        @pl.loop(1, n)
        def _(s):
            part_copy(c, s, lax.rem(me + n - s, n), me).wait_recv()

        cut = slice(c * turn_groups, (c + 1) * turn_groups)
        totals, squares = parts[c, :, 0], parts[c, :, 1]
        average = jnp.sum(totals, axis=0) / samples
        away = totals / LANES - average[None]
        variance = (jnp.sum(squares, axis=0) + LANES * jnp.sum(away * away, axis=0)) / samples
        width = width_rows[cut, :]
        res_ref[0, cut, :] = width * average
        res_ref[1, cut, :] = 1.0 / jnp.sqrt(width * (variance + 1e-05))

    for c in range(turns):

        @pl.loop(1, n)
        def _(s):
            part_copy(c, s, me, lax.rem(me + s, n)).wait_send()

    @pl.loop(1, n)
    def _(s):
        slab_copy(s, me, lax.rem(me + s, n)).wait_send()


def norm_kernel(box_in, res_ref, out_ref, box_ref, done, load_sems, sems):
    groups = res_ref.shape[1]
    per_group = box_ref.shape[0] // groups
    loads, copies = [], []
    for g in range(groups):
        rows = slice(g * per_group, (g + 1) * per_group)
        loads.append(pltpu.make_async_copy(box_in.at[rows], box_ref.at[rows], load_sems.at[g]))
        loads[-1].start()
    for g in range(groups):
        rows = slice(g * per_group, (g + 1) * per_group)
        base, scale = (
            jnp.broadcast_to(res_ref[i, g : g + 1, :], (LANES, LANES)).T[:per_group]
            for i in range(2)
        )
        loads[g].wait()
        done[rows, :] = (box_ref[rows, :] - base) * scale
        copies.append(pltpu.make_async_copy(done.at[rows], out_ref.at[rows], sems.at[g]))
        copies[-1].start()
    for copy in copies:
        copy.wait()


def per_device(filterbank, chan_delay, sub_delay, widths):
    chan_count, samples = filterbank.shape
    groups = chan_delay.shape[0]
    n = lax.axis_size("gx")
    trials, bands = sub_delay.shape
    per_group = trials // groups
    bands_here = chan_count // SUBCH
    assert samples == n * LANES and n >= groups and chan_count == LANES
    message_rows = (bands_here + 1) * groups
    offsets = DELAY_TWO + WMAX
    slot_bytes = 2 * per_group * offsets * bands * 2
    slots = groups if groups * slot_bytes <= PREBUILD_BYTES else 1
    turn_groups = min(8, groups)
    turns = groups // turn_groups
    rep = max(1, LANES // bands)
    bf16, f32, i32 = jnp.bfloat16, jnp.float32, jnp.int32
    arrays = [
        ((chan_count, samples), bf16),
        ((groups, chan_count), i32),
        ((bands, trials), i32),
        ((trials,), i32),
        ((trials, rep * bands), i32),
        ((trials, LANES), i32),
        ((groups, LANES), f32),
        ((n, message_rows, LANES), bf16),
        ((n, message_rows, LANES), bf16),
        ((groups, bands, LANES), bf16),
        ((groups, bands, LANES), bf16),
        ((slots, 2 * per_group, offsets * bands), bf16),
        ((turns, n, 2, turn_groups, LANES), f32),
        ((turns, 2, turn_groups, LANES), f32),
    ]
    held = sum(math.prod(shape) * jnp.dtype(kind).itemsize for shape, kind in arrays)
    vmem = pl.BlockSpec(memory_space=pltpu.VMEM)
    anywhere = pl.BlockSpec(memory_space=pl.ANY)
    dma = pltpu.SemaphoreType.DMA
    boxcar, stats = pl.pallas_call(
        functools.partial(main_kernel, n),
        out_shape=(
            jax.ShapeDtypeStruct((trials, LANES), f32),
            jax.ShapeDtypeStruct((2, groups, LANES), f32),
        ),
        in_specs=[anywhere] * 4,
        out_specs=(vmem, vmem),
        scratch_shapes=[pltpu.VMEM(shape, kind) for shape, kind in arrays]
        + [dma((4,)), dma((n,)), dma((n,)), dma((turns, n)), dma((turns, n))],
        compiler_params=pltpu.CompilerParams(
            collective_id=0, has_side_effects=True, vmem_limit_bytes=max(56 << 20, held + (10 << 20))
        ),
        name="dedisperse",
    )(filterbank, chan_delay, sub_delay.T, widths)
    return pl.pallas_call(
        norm_kernel,
        out_shape=jax.ShapeDtypeStruct((trials, LANES), f32),
        in_specs=[anywhere, vmem],
        out_specs=anywhere,
        scratch_shapes=[pltpu.VMEM((trials, LANES), f32)] * 2 + [dma((groups,))] * 2,
        compiler_params=pltpu.CompilerParams(vmem_limit_bytes=56 << 20),
        name="normalise",
    )(boxcar, stats)


def solution(mesh):
    in_specs = (P(("beam", "gx"), None), P(None, "gx"), P(), P())
    out_specs = P("beam", "gx")
    return jax.shard_map(
        per_device, mesh=mesh, in_specs=in_specs, out_specs=out_specs, check_vma=False
    )
```

time: 39.9 us -> 35 us (0.88)
  local copies, waits for them, and re-layouts: 3.31 us -> 0 us
  Pallas kernels: 36.4 us -> 34.7 us
    pallas_call x1, Pallas kernels: 33.8 us -> 30.9 us  [per_device(): pl.pallas_call(functools.partial(main_kernel, n), out_shape=(jax.ShapeDty...]
    unnamed x3 -> x0, local copies, waits for them, and re-layouts: 2.16 us -> none
    pallas_call x1, Pallas kernels: 2.61 us -> 3.81 us  [per_device(): pl.pallas_call(norm_kernel, out_shape=jax.ShapeDtypeStruct((trials, LANES...]
    broadcast_in_dim x1 -> x0, local copies, waits for them, and re-layouts: 1.15 us -> none  [per_device(): wide = jnp.broadcast_to(widths[:, None], (trials, LANES))]
where the time goes in v2:
time: 35 us; the launch traced here: 34.7 us
  Pallas kernels  34.7 us (99%)
    pallas_call x1, Pallas kernels, per_device(): pl.pallas_call(functools.partial(main_kernel, n), out_shape=(jax.ShapeDty...  30.9 us
    pallas_call x1, Pallas kernels, per_device(): pl.pallas_call(norm_kernel, out_shape=jax.ShapeDtypeStruct((trials, LANES...  3.81 us

profile of v2, /device:TPU:0, one launch (start us, length us, event | category | flops | bytes accessed | tf_op | source)
XLA Modules:
  0.0 34.7 jit_solution(9940088192370344263)
XLA Ops:
  0.0 30.9 %dedisperse.1 = (f32[1536,128]{1,0:T(8,128)}, f32[2,16,128]{2,1,0:T(8,128)}) custom-call(bf16[128,2048]{1,0:T(8,128)(2,1)} %fb_in.1, s32[16,128]{1,0:T(8,128)} %cd_in.1, s32[64,1536]{1,0:T(8,128)} %bitcast.1, s32[1536]{0:T(1024)} %w_in.1), custom_call_target="tpu_custom_call" | custom-call | tf_op jit(solution)/shard_map/dedisperse/pallas_call | solution.py:356
  30.9 3.8 %normalise.1 = f32[1536,128]{1,0:T(8,128)} custom-call(f32[1536,128]{1,0:T(8,128)} %get-tuple-element.7.box_in, f32[2,16,128]{2,1,0:T(8,128)} %get-tuple-element.8.res_ref), custom_call_target="tpu_custom_call" | custom-call | tf_op jit(solution)/shard_map/normalise/pallas_call | solution.py:371

commit v3 on v2

--- a/solution.py
+++ b/solution.py
@@ -35,7 +35,6 @@
     sd_in,
     w_in,
     box_ref,
-    res_ref,
     fb_ref,
     cd_ref,
     sd_ref,
@@ -50,6 +49,7 @@
     lhs,
     parts,
     mine,
+    res_ref,
     load_sem,
     send_sem,
     recv_sem,
@@ -114,7 +114,7 @@
 
     loads[1].wait()
 
-    @pl.loop(0, tiles // 2)
+    @pl.loop(0, tiles // 2, unroll=4)
     def _(pair):
         first, second = tile(2 * pair), tile(2 * pair + 1)
         third = tile(jnp.minimum(2 * pair + 2, tiles - 1))
@@ -189,7 +189,7 @@
         in_row == (out_row & (ROWS - 1)) * groups + (out_row >> 4), 1.0, 0.0
     ).astype(bf16)
 
-    @pl.loop(0, n // per_pack)
+    @pl.loop(0, n // per_pack, unroll=4)
     def _(q):
         mains, halos = [], []
         for s in range(per_pack):
@@ -246,7 +246,7 @@
 
     for c in range(turns):
 
-        @pl.loop(0, turn_groups)
+        @pl.loop(0, turn_groups, unroll=8)
         def _(r):
             g = c * turn_groups + r
             both = summed(g, 2 * per_group, range(0, DELAY_TWO, chunk))
@@ -264,7 +264,7 @@
 
         parts[c, me] = mine[c]
 
-    @pl.loop(0, groups)
+    @pl.loop(0, groups, unroll=8)
     def _(g):
         upper = summed(g, per_group, range(DELAY_TWO, DELAY_TWO + WMAX, chunk))
         box_ref[rows_of(g), :] = box_ref[rows_of(g), :] + upper
@@ -284,6 +284,17 @@
         res_ref[0, cut, :] = width * average
         res_ref[1, cut, :] = 1.0 / jnp.sqrt(width * (variance + 1e-05))
 
+    @pl.loop(0, groups // 4)
+    def _(q):
+        for r in range(4):
+            g = q * 4 + r
+            rows = rows_of(g)
+            base, scale = (
+                jnp.broadcast_to(res_ref[i, pl.ds(g, 1), :], (LANES, LANES)).T[:per_group]
+                for i in range(2)
+            )
+            box_ref[rows, :] = (box_ref[rows, :] - base) * scale
+
     for c in range(turns):
 
         @pl.loop(1, n)
@@ -293,28 +304,6 @@
     @pl.loop(1, n)
     def _(s):
         slab_copy(s, me, lax.rem(me + s, n)).wait_send()
-
-
-def norm_kernel(box_in, res_ref, out_ref, box_ref, done, load_sems, sems):
-    groups = res_ref.shape[1]
-    per_group = box_ref.shape[0] // groups
-    loads, copies = [], []
-    for g in range(groups):
-        rows = slice(g * per_group, (g + 1) * per_group)
-        loads.append(pltpu.make_async_copy(box_in.at[rows], box_ref.at[rows], load_sems.at[g]))
-        loads[-1].start()
-    for g in range(groups):
-        rows = slice(g * per_group, (g + 1) * per_group)
-        base, scale = (
-            jnp.broadcast_to(res_ref[i, g : g + 1, :], (LANES, LANES)).T[:per_group]
-            for i in range(2)
-        )
-        loads[g].wait()
-        done[rows, :] = (box_ref[rows, :] - base) * scale
-        copies.append(pltpu.make_async_copy(done.at[rows], out_ref.at[rows], sems.at[g]))
-        copies[-1].start()
-    for copy in copies:
-        copy.wait()
 
 
 def per_device(filterbank, chan_delay, sub_delay, widths):
@@ -348,19 +337,17 @@
         ((slots, 2 * per_group, offsets * bands), bf16),
         ((turns, n, 2, turn_groups, LANES), f32),
         ((turns, 2, turn_groups, LANES), f32),
+        ((2, groups, LANES), f32),
     ]
     held = sum(math.prod(shape) * jnp.dtype(kind).itemsize for shape, kind in arrays)
     vmem = pl.BlockSpec(memory_space=pltpu.VMEM)
     anywhere = pl.BlockSpec(memory_space=pl.ANY)
     dma = pltpu.SemaphoreType.DMA
-    boxcar, stats = pl.pallas_call(
+    return pl.pallas_call(
         functools.partial(main_kernel, n),
-        out_shape=(
-            jax.ShapeDtypeStruct((trials, LANES), f32),
-            jax.ShapeDtypeStruct((2, groups, LANES), f32),
-        ),
+        out_shape=jax.ShapeDtypeStruct((trials, LANES), f32),
         in_specs=[anywhere] * 4,
-        out_specs=(vmem, vmem),
+        out_specs=vmem,
         scratch_shapes=[pltpu.VMEM(shape, kind) for shape, kind in arrays]
         + [dma((4,)), dma((n,)), dma((n,)), dma((turns, n)), dma((turns, n))],
         compiler_params=pltpu.CompilerParams(
@@ -368,16 +355,6 @@
         ),
         name="dedisperse",
     )(filterbank, chan_delay, sub_delay.T, widths)
-    return pl.pallas_call(
-        norm_kernel,
-        out_shape=jax.ShapeDtypeStruct((trials, LANES), f32),
-        in_specs=[anywhere, vmem],
-        out_specs=anywhere,
-        scratch_shapes=[pltpu.VMEM((trials, LANES), f32)] * 2 + [dma((groups,))] * 2,
-        compiler_params=pltpu.CompilerParams(vmem_limit_bytes=56 << 20),
-        name="normalise",
-    )(boxcar, stats)
-
 
 def solution(mesh):
     in_specs = (P(("beam", "gx"), None), P(None, "gx"), P(), P())

time: 35 us -> 29.2 us (0.83)
  Pallas kernels: 34.7 us -> 26.9 us
  local copies, waits for them, and re-layouts: 0 us -> 2.06 us
    pallas_call x2 -> x1, Pallas kernels: 34.7 us -> 26.9 us  [per_device(): pl.pallas_call(functools.partial(main_kernel, n), out_shape=jax.ShapeDtyp...]
    unnamed x0 -> x1, local copies, waits for them, and re-layouts: none -> 2.06 us
where the time goes in v3:
time: 29.2 us; the launch traced here: 29 us
  Pallas kernels  26.9 us (92%)
  local copies, waits for them, and re-layouts  2.06 us (7%)
    pallas_call x1, Pallas kernels, per_device(): pl.pallas_call(functools.partial(main_kernel, n), out_shape=jax.ShapeDtyp...  26.9 us
    unnamed x1, local copies, waits for them, and re-layouts  2.06 us

profile of v3, /device:TPU:0, one launch (start us, length us, event | category | flops | bytes accessed | tf_op | source)
XLA Modules:
  0.0 29.0 jit_solution(15403813147891284703)
XLA Ops:
  0.0 26.9 %dedisperse.1 = f32[1536,128]{1,0:T(8,128)} custom-call(bf16[128,2048]{1,0:T(8,128)(2,1)} %fb_in.1, s32[16,128]{1,0:T(8,128)} %cd_in.1, s32[64,1536]{1,0:T(8,128)} %bitcast.1, s32[1536]{0:T(1024)} %w_in.1), custom_call_target="tpu_custom_call" | custom-call | tf_op jit(solution)/shard_map/dedisperse/pallas_call | solution.py:346
  26.9 2.1 %copy.6 = f32[1536,128]{1,0:T(8,128)} copy(f32[1536,128]{1,0:T(8,128)} %dedisperse.1) | data formatting | bytes 1572864
